TPU v7x, 512 devices: a whole 4x4x16 slice. The times are simulated.
512 devices in a mesh: row: 32 (over x, y, core), col: 16 (over z).
Axes of the slice: x: 4, y: 4, z: 16, core: 2. Of those that a mesh axis runs over, the one named last changes fastest.
Arguments:
- tokens: bfloat16 [256, 8192], P('row', 'col'), may hold values from -6 to 6
- gate_weight: bfloat16 [8192, 24576], P('col', 'row'), may hold values from -0.0625 to 0.0625
- up_weight: bfloat16 [8192, 24576], P('col', 'row'), may hold values from -0.0625 to 0.0625
- down_weight: bfloat16 [24576, 8192], P('row', 'col'), may hold values from -0.0390625 to 0.0390625
- out_grad: bfloat16 [256, 8192], P('row', 'col'), may hold values from -1.5 to 1.5
Outputs:
- mixed: bfloat16 [256, 8192], P('row', 'col')
- input_grad: bfloat16 [256, 8192], P('row', 'col')
- gate_grad: bfloat16 [8192, 24576], P('col', 'row')
- up_grad: bfloat16 [8192, 24576], P('col', 'row')
- down_grad: bfloat16 [24576, 8192], P('row', 'col')
All inputs are finite; a program needn't handle non-finite values.
Results may differ from a plain program's by a relative error of at most 0.0049.
Values may be sent and summed in bfloat16 or wider, within the bound.
A program may use at most 64 MiB of HBM per device.

v0:
```python
import jax
import jax.numpy as jnp
from jax import lax
from jax.sharding import PartitionSpec as P


def reduce_rows(term_fn, total_rows, rows):
    summed = lax.psum(term_fn(0, total_rows), "row")
    return lax.dynamic_slice_in_dim(summed, lax.axis_index("row") * rows, rows, 0)


def shards(tokens, gate_weight, up_weight, down_weight, out_grad):
    rows = tokens.shape[0]
    all_tokens, all_grads = (
        lax.all_gather(tokens, "row", axis=0, tiled=True),
        lax.all_gather(out_grad, "row", axis=0, tiled=True),
    )
    total_rows = all_tokens.shape[0]
    units = gate_weight.shape[1]
    joined_weight = jnp.concatenate([gate_weight, up_weight], axis=1)
    back = (((1,), (1,)), ((), ()))
    contract = (((0,), (0,)), ((), ()))
    block = all_tokens
    gate_up = lax.psum_scatter(
        jnp.dot(block, joined_weight, preferred_element_type=jnp.float32),
        "col",
        scatter_dimension=0,
        tiled=True,
    )
    gate = gate_up[:, :units]
    up_value = gate_up[:, units:]
    sigmoid = jax.nn.sigmoid(gate)
    swish = gate * sigmoid
    hidden_mine = (swish * up_value).astype(jnp.bfloat16)
    hidden = lax.all_gather(hidden_mine, "col", axis=0, tiled=True)

    def output_term(start, count):
        return jnp.dot(hidden, down_weight, preferred_element_type=jnp.float32)

    mixed = reduce_rows(output_term, total_rows, rows).astype(jnp.bfloat16)
    down_grad = lax.dot_general(
        hidden, all_grads, contract, preferred_element_type=jnp.float32
    ).astype(jnp.bfloat16)
    block = all_grads
    hidden_grad = lax.psum_scatter(
        lax.dot_general(block, down_weight, back, preferred_element_type=jnp.float32),
        "col",
        scatter_dimension=0,
        tiled=True,
    )
    gate_delta = (hidden_grad * up_value * sigmoid * (1.0 + gate * (1.0 - sigmoid))).astype(
        jnp.bfloat16
    )
    up_delta = (hidden_grad * swish).astype(jnp.bfloat16)
    gate_rows, up_rows = (
        lax.all_gather(gate_delta, "col", axis=0, tiled=True),
        lax.all_gather(up_delta, "col", axis=0, tiled=True),
    )
    deltas = jnp.concatenate([gate_rows, up_rows], axis=1)
    weight_grads = lax.dot_general(all_tokens, deltas, contract, preferred_element_type=jnp.float32)
    gate_grad = weight_grads[:, :units].astype(jnp.bfloat16)
    up_grad = weight_grads[:, units:].astype(jnp.bfloat16)

    def input_term(start, count):
        return lax.dot_general(deltas, joined_weight, back, preferred_element_type=jnp.float32)

    input_grad = reduce_rows(input_term, total_rows, rows).astype(jnp.bfloat16)
    return (mixed, input_grad, gate_grad, up_grad, down_grad)


def solution(mesh):
    return jax.shard_map(
        shards,
        mesh=mesh,
        in_specs=(
            P("row", "col"),
            P("col", "row"),
            P("col", "row"),
            P("row", "col"),
            P("row", "col"),
        ),
        out_specs=(
            P("row", "col"),
            P("row", "col"),
            P("col", "row"),
            P("col", "row"),
            P("row", "col"),
        ),
        check_vma=False,
    )
```

profile of v0, /device:TPU:1, one launch (start us, length us, event | category | flops | bytes accessed | tf_op | source)
XLA Modules:
  0.0 411.9 jit_solution(11833059371363956905)
XLA Ops:
  7.2 0.0 copy-start
  7.2 0.0 copy-start.2
  7.2 0.0 reduce-scatter.9.cloned.1.call-start
  7.2 29.3 %all_gather.17 = bf16[256,512]{1,0:T(8,128)(2,1)S(1)} all-gather(bf16[8,512]{1,0:T(8,128)(2,1)} %param.9), channel_id=1, replica_groups=mesh['row'=32,'col'=16] {'row'}, dimensions={0}, use_global_device_ids=true | all-gather | bytes 270336 | tf_op jit(solution)/shard_map/all_gather | solution.py:16
  36.5 0.0 copy-done
  36.5 1.3 fusion.4
  37.8 0.0 reduce-scatter.9.cloned.1.call-update
  37.8 0.0 reduce-scatter.7.cloned.1.call-start
  37.9 0.0 copy-done.2
  37.9 24.3 %all_gather.15 = bf16[256,512]{1,0:T(8,128)(2,1)S(1)} all-gather(bf16[8,512]{1,0:T(8,128)(2,1)S(1)} %copy-done.2), channel_id=1, replica_groups=mesh['row'=32,'col'=16] {'row'}, dimensions={0}, use_global_device_ids=true | all-gather | bytes 270336 | tf_op jit(solution)/shard_map/all_gather | solution.py:15
  62.1 1.2 constant_dynamic-update-slice_fusion.1
  63.3 1.2 constant_dynamic-update-slice_fusion
  64.5 1.8 convolution_bitcast_fusion
  66.3 3.1 copy.27
  69.4 0.0 reduce-scatter.7.cloned.1.call-update
  69.4 27.1 %reduce-scatter.9.cloned.1.call-done = f32[16,768]{1,0:T(8,128)} async-done(((f32[256,768]{1,0:T(8,128)}), f32[16,768]{1,0:T(8,128)}) %reduce-scatter.9.cloned.1.call-update) | async-done | bytes 49168 | tf_op jit(solution)/shard_map/reduce_scatter | solution.py:45
  96.5 72.6 %reduce-scatter.7.cloned.1.call-done = f32[16,1536]{1,0:T(8,128)} async-done(((f32[256,1536]{1,0:T(8,128)}), f32[16,1536]{1,0:T(8,128)}) %reduce-scatter.7.cloned.1.call-update) | async-done | bytes 98320 | tf_op jit(solution)/shard_map/reduce_scatter | solution.py:24
  169.1 0.9 multiply_convert_fusion
  170.0 23.7 %all_gather.18 = bf16[256,768]{1,0:T(8,128)(2,1)S(1)} all-gather(bf16[16,768]{1,0:T(8,128)(2,1)S(1)} %get-tuple-element.25), channel_id=1, replica_groups=mesh['row'=32,'col'=16] {'col'}, dimensions={0}, use_global_device_ids=true | all-gather | bytes 417792 | tf_op jit(solution)/shard_map/all_gather | solution.py:56
  193.7 22.0 %all_gather.19 = bf16[256,768]{1,0:T(8,128)(2,1)S(1)} all-gather(bf16[16,768]{1,0:T(8,128)(2,1)S(1)} %get-tuple-element.24), channel_id=1, replica_groups=mesh['row'=32,'col'=16] {'col'}, dimensions={0}, use_global_device_ids=true | all-gather | bytes 417792 | tf_op jit(solution)/shard_map/all_gather | solution.py:57
  215.7 1.4 fusion.5
  217.1 0.6 fusion
  217.7 23.1 %all_gather.16 = bf16[256,768]{1,0:T(8,128)(2,1)S(1)} all-gather(bf16[16,768]{1,0:T(8,128)(2,1)S(1)} %get-tuple-element.26), channel_id=1, replica_groups=mesh['row'=32,'col'=16] {'col'}, dimensions={0}, use_global_device_ids=true | all-gather | bytes 417792 | tf_op jit(solution)/shard_map/all_gather | solution.py:35
  240.8 0.4 fusion.3
  241.2 1.3 convolution_convert_fusion.1
  242.4 0.1 fusion.2
  242.6 1.2 copy.24
  243.7 0.0 copy-start.1
  243.7 1.2 copy.25
  244.9 0.0 copy-done.1
  244.9 159.6 %all-reduce.2 = (bf16[256,512]{1,0:T(8,128)(2,1)S(1)}, bf16[256,512]{1,0:T(8,128)(2,1)S(1)}) all-reduce(f32[256,512]{1,0:T(8,128)S(1)} %fusion.3, f32[256,512]{1,0:T(8,128)S(1)} %copy-done.1), channel_id=1, replica_groups=mesh['row'=32,'col'=16] {'row'}, use_global_device_ids=true, to_apply=%region_1.0 | all-reduce | flops 262144 | bytes 1572864 | tf_op jit(solution)/shard_map/psum | solution.py:8
  404.5 0.6 dynamic-slice_convert_fusion
  (2 shorter events, 0.1 us)
Async XLA Ops:
  7.2 29.3 %copy-start = (bf16[768,512]{1,0:T(8,128)(2,1)S(1)}, bf16[768,512]{1,0:T(8,128)(2,1)}, u32[]{:S(2)}) copy-start(bf16[768,512]{1,0:T(8,128)(2,1)} %param.8) | copy-start | bytes 2359300
  7.2 30.7 %copy-start.2 = (bf16[8,512]{1,0:T(8,128)(2,1)S(1)}, bf16[8,512]{1,0:T(8,128)(2,1)}, u32[]{:S(2)}) copy-start(bf16[8,512]{1,0:T(8,128)(2,1)} %param.5) | copy-start | bytes 24580
  7.2 89.3 %reduce-scatter.9.cloned.1.call-start = ((), (), s32[]{:S(2)}) async-start(), calls=%async_computation.3 | async-start | bytes 835584 | tf_op jit(solution)/shard_map/reduce_scatter | solution.py:45
  37.8 131.3 %reduce-scatter.7.cloned.1.call-start = ((), (), s32[]{:S(2)}) async-start(), calls=%async_computation.2 | async-start | bytes 1671168 | tf_op jit(solution)/shard_map/reduce_scatter | solution.py:24
  243.7 1.2 copy-start.1
Sparse Core Ops, SparseCore 0:
  37.9 58.5 reduce-scatter.8
  99.6 69.5 reduce-scatter.6
where the time goes:
time: 415 us; the launch traced here: 412 us
  blocking collectives  282 us (68%)
  waiting for transfers between devices  99.8 us (24%)
  between operations  14.1 us (3%)
  local copies, waits for them, and re-layouts  8.53 us (2%)
  matrix products  6.7 us (2%)
    psum x1, blocking collectives, reduce_rows(): summed = lax.psum(term_fn(0, total_rows), 'row')  160 us
    reduce_scatter x1, waiting for transfers between devices, shards(): lax.psum_scatter(jnp.dot(block, joined_weight, preferred_element_type=jnp...  72.6 us
    all_gather x1, blocking collectives, shards(): lax.all_gather(out_grad, 'row', axis=0, tiled=True)  29.3 us
    reduce_scatter x1, waiting for transfers between devices, shards(): lax.psum_scatter(lax.dot_general(block, down_weight, back, preferred_elem...  27.1 us
    all_gather x1, blocking collectives, shards(): lax.all_gather(tokens, 'row', axis=0, tiled=True)  24.3 us
    all_gather x1, blocking collectives, shards(): lax.all_gather(gate_delta, 'col', axis=0, tiled=True)  23.7 us
    all_gather x1, blocking collectives, shards(): hidden = lax.all_gather(hidden_mine, 'col', axis=0, tiled=True)  23.1 us
    all_gather x1, blocking collectives, shards(): lax.all_gather(up_delta, 'col', axis=0, tiled=True)  22 us
  transfers between devices with their start and end apart: 2, of which 2 were waited for; matrix products, arithmetic and copies ran while one was open for 2% of the time, Pallas kernels for 0%

commit v1 on v0

v1 whole, which is shorter than its diff:
```python
import functools

import jax
import jax.numpy as jnp
from jax import lax
from jax.experimental import pallas as pl
from jax.experimental.pallas import tpu as pltpu
from jax.sharding import PartitionSpec as P

MESH = pl.DeviceIdType.MESH
F32, BF16 = jnp.float32, jnp.bfloat16
NZ, NX, NY = 16, 4, 4
LANES, W = 3, 256

RIGHT = {1: 0, 2: 1, 3: 2, 4: 3, 5: 4, 6: 5, 7: 6, 8: 7}
LEFT = {-1: 0, -2: -1, -3: -2, -4: -3, -5: -4, -6: -5, -7: -6}
SUM_TREES = [{**RIGHT, **LEFT}] * LANES
SPREAD_TREES = [{**RIGHT, **LEFT}] * LANES


def mirrored(tree):
    return {-k: -p for k, p in tree.items()}


def children(tree, k):
    return [c for c, p in tree.items() if p == k]


def plan(sum_trees, spread_trees, sum_kb=48.0, spread_kb=24.0):
    free = {1: 0.0, -1: 0.0}
    arrive = {}
    clock = 0.0
    order = []

    def send(key, dist, kb, now):
        way = 1 if dist > 0 else -1
        hops = abs(dist)
        wire = kb * 2 * hops / 112.0
        begin = max(free[way], now)
        free[way] = begin + wire
        arrive[key] = begin + wire + 2.2 + 0.6 * hops

    todo = []
    for u in range(LANES):
        todo.append(("mm", u, 0))
        todo += [("sum", u, k) for k in sum_trees[u]]
        todo.append(("own", u, 0))
        todo += [("spread", u, k) for k in spread_trees[u] if children(spread_trees[u], k)]
        todo.append(("fin", u, 0))
        todo.append(("grad", u, 0))
    done = set()
    cost = {"mm": 0.8, "sum": 0.15, "own": 0.4, "spread": 0.08, "fin": 0.8, "grad": 0.9}
    last = {"mm": 0, "grad": 1e6}

    def ready(task):
        kind, u, k = task
        if kind == "mm":
            return 0.0 if u == 0 or ("mm", u - 1, 0) in done else None
        if kind == "sum" or kind == "own":
            if ("mm", u, 0) not in done:
                return None
            keys = [("sum", u, c) for c in children(sum_trees[u], k)]
        elif kind == "spread":
            keys = [("spread", u, k)]
        elif kind == "fin":
            if ("own", u, 0) not in done:
                return None
            keys = [("spread", u, c) for c in spread_trees[u]]
        else:
            return 0.0 if ("fin", u, 0) in done else None
        if any(key not in arrive for key in keys):
            return None
        return max([0.0] + [arrive[key] for key in keys])

    while todo:
        best = None
        for task in todo:
            at = ready(task)
            if at is None:
                continue
            rank = (max(at, clock) + last.get(task[0], 0.0) * 1.0, task[1], at)
            if best is None or rank < best[0]:
                best = (rank, task, at)
        _, task, at = best
        kind, u, k = task
        clock = max(clock, at) + cost[kind]
        if kind == "sum":
            send(("sum", u, k), k - sum_trees[u][k], sum_kb, clock)
        elif kind in ("own", "spread"):
            for c in children(spread_trees[u], k):
                send(("spread", u, c), c - k, spread_kb, clock)
        order.append(task)
        done.add(task)
        todo.remove(task)
    return order, clock


def offsets(sum_trees, spread_trees):
    found = set()
    for tree in sum_trees:
        found |= {(k - p) % NZ for k, p in tree.items()}
    for tree in spread_trees:
        found |= {(k - p) % NZ for k, p in tree.items()}
    found |= {(-o) % NZ for o in found}
    return sorted(found)


def torus(step):
    return min(step, 4 - step)


STEPS = sorted(
    [(dx, dy) for dx in range(NX) for dy in range(NY) if (dx, dy) != (0, 0)],
    key=lambda s: -(torus(s[0]) + torus(s[1])),
)
COLUMNS = [0, 1, 3, 2]


def dot(a, b, dims):
    return lax.dot_general(a, b, (dims, ((), ())), preferred_element_type=F32)


NN, NT, TN = ((1,), (0,)), ((1,), (1,)), ((0,), (0,))


def kernel(
    sum_trees, spread_trees, order,
    tok, gate_w, up_w, down_w, og,
    mixed, input_grad, gate_grad, up_grad, down_grad,
    gw, uw, dw, slabs, xs, gs, part, slot, acts, halves, sib, dsend, drecv, gg, ug, dg,
    w_sem, out_sem, a_send, a_recv, f_send, f_recv,
    sum_send, sum_recv, spread_send, spread_recv, h_send, h_recv, d_send, d_recv,
):
    row, z = lax.axis_index("row"), lax.axis_index("col")
    core, chip = row % 2, row // 2
    x, y = chip // NY, chip % NY
    sibling = (chip * 2 + 1 - core, z)

    loads = [
        pltpu.make_async_copy(src, dst, w_sem.at[i])
        for i, (src, dst) in enumerate(((gate_w, gw), (up_w, uw), (down_w, dw)))
    ]
    for load in loads:
        load.start()

    def plane(dx, dy):
        return ((x + dx) % NX) * NY + (y + dy) % NY

    barrier = pltpu.get_barrier_semaphore()
    around = offsets(sum_trees, spread_trees)
    for dx, dy in STEPS:
        pl.semaphore_signal(
            barrier, inc=1, device_id=(plane(dx, dy) * 2 + core, z), device_id_type=MESH
        )
    for o in around:
        pl.semaphore_signal(barrier, inc=1, device_id=(row, (z + o) % NZ), device_id_type=MESH)
    pl.semaphore_signal(barrier, inc=1, device_id=sibling, device_id_type=MESH)
    slabs[core, x, y] = jnp.concatenate(
        [tok[...].astype(F32), og[...].astype(F32)], axis=0
    ).astype(BF16)
    pl.semaphore_wait(barrier, len(STEPS) + len(around) + 1)

    def gather(dx, dy, from_x, from_y):
        return pltpu.make_async_remote_copy(
            src_ref=slabs.at[core, from_x, from_y],
            dst_ref=slabs.at[core, from_x, from_y],
            send_sem=a_send.at[dx * NY + dy],
            recv_sem=a_recv.at[dx * NY + dy],
            device_id=(plane(dx, dy) * 2 + core, z),
            device_id_type=MESH,
        )

    def forward(dx, which):
        return pltpu.make_async_remote_copy(
            src_ref=slabs.at[which, (x - dx) % NX],
            dst_ref=slabs.at[which, (x - dx) % NX],
            send_sem=f_send.at[dx],
            recv_sem=f_recv.at[dx],
            device_id=sibling,
            device_id_type=MESH,
        )

    for dx, dy in STEPS:
        gather(dx, dy, x, y).start()
    for dx in COLUMNS:
        for dy in range(NY):
            if (dx, dy) != (0, 0):
                gather(dx, dy, (x - dx) % NX, (y - dy) % NY).wait_recv()
        forward(dx, core).start()
    for load in loads:
        load.wait()
    for dx in COLUMNS:
        forward(dx, 1 - core).wait_recv()
    both = slabs[...].astype(F32)
    xs[...] = both[:, :, :, 0:8, :].reshape(256, 512).astype(BF16)
    gs[...] = both[:, :, :, 8:16, :].reshape(256, 512).astype(BF16)

    index = {k: i for i, k in enumerate(sorted(sum_trees[0]))}

    def sum_copy(u, k):
        o = k - sum_trees[u][k]
        return pltpu.make_async_remote_copy(
            src_ref=part.at[u, (z + k) % NZ],
            dst_ref=slot.at[u, index[k]],
            send_sem=sum_send.at[u, index[k]],
            recv_sem=sum_recv.at[u, index[k]],
            device_id=(row, (z + o) % NZ),
            device_id_type=MESH,
        )

    def spread_copy(u, c, chunk):
        o = c - spread_trees[u][c]
        return pltpu.make_async_remote_copy(
            src_ref=acts.at[u, chunk],
            dst_ref=acts.at[u, chunk],
            send_sem=spread_send.at[u, index[c]],
            recv_sem=spread_recv.at[u, index[c]],
            device_id=(row, (z + o) % NZ),
            device_id_type=MESH,
        )

    def spread_wait(u, k):
        spread_copy(u, k, (z - k) % NZ).wait_recv()

    for kind, u, k in order:
        unit = pl.ds(u * W, W)
        if kind == "mm":
            part[u, :, :, 0:W] = dot(xs[...], gw[:, unit], NN).reshape(NZ, 16, W)
            part[u, :, :, W : 2 * W] = dot(xs[...], uw[:, unit], NN).reshape(NZ, 16, W)
            part[u, :, :, 2 * W : 3 * W] = dot(gs[...], dw[unit, :], NT).reshape(NZ, 16, W)
        elif kind == "sum":
            below = children(sum_trees[u], k)
            if below:
                chunk = (z + k) % NZ
                total = part[u, chunk]
                for c in below:
                    sum_copy(u, c).wait_recv()
                    total += slot[u, index[c]]
                part[u, chunk] = total
            sum_copy(u, k).start()
        elif kind == "own":
            total = part[u, z]
            for c in children(sum_trees[u], 0):
                sum_copy(u, c).wait_recv()
                total += slot[u, index[c]]
            gate, up, hidden_grad = total[:, 0:W], total[:, W : 2 * W], total[:, 2 * W :]
            sig = jax.nn.sigmoid(gate)
            swish = gate * sig
            acts[u, z, :, 0:W] = (swish * up).astype(BF16)
            acts[u, z, :, W : 2 * W] = (
                hidden_grad * up * sig * (1.0 + gate * (1.0 - sig))
            ).astype(BF16)
            acts[u, z, :, 2 * W : 3 * W] = (hidden_grad * swish).astype(BF16)
            for c in children(spread_trees[u], 0):
                spread_copy(u, c, z).start()
        elif kind == "spread":
            spread_wait(u, k)
            for c in children(spread_trees[u], k):
                spread_copy(u, c, (z - k) % NZ).start()
        elif kind == "fin":
            for c in spread_trees[u]:
                if not children(spread_trees[u], c):
                    spread_wait(u, c)
            hidden = acts[u, :, :, 0:W].reshape(256, W)
            gate_delta = acts[u, :, :, W : 2 * W].reshape(256, W)
            up_delta = acts[u, :, :, 2 * W : 3 * W].reshape(256, W)
            out = dot(hidden, dw[unit, :], NN).reshape(2, 16, 8, 512)
            back = (dot(gate_delta, gw[:, unit], NT) + dot(up_delta, uw[:, unit], NT)).reshape(
                2, 16, 8, 512
            )
            if u != LANES_FIRST:
                out += halves[:, :, 0:8, :]
                back += halves[:, :, 8:16, :]
            halves[:, :, 0:8, :] = out
            halves[:, :, 8:16, :] = back
        else:
            hidden = acts[u, :, :, 0:W].reshape(256, W)
            gate_delta = acts[u, :, :, W : 2 * W].reshape(256, W)
            up_delta = acts[u, :, :, 2 * W : 3 * W].reshape(256, W)
            gg[:, unit] = dot(xs[...], gate_delta, TN).astype(BF16)
            ug[:, unit] = dot(xs[...], up_delta, TN).astype(BF16)
            dg[unit, :] = dot(hidden, gs[...], TN).astype(BF16)
        if kind == "fin" and (kind, u, k) == [t for t in order if t[0] == "fin"][-1]:
            half = pltpu.make_async_remote_copy(
                src_ref=halves.at[1 - core],
                dst_ref=sib,
                send_sem=h_send,
                recv_sem=h_recv,
                device_id=sibling,
                device_id_type=MESH,
            )
            half.start()
            half.wait_recv()

            def scatter(dx, dy):
                return pltpu.make_async_remote_copy(
                    src_ref=dsend.at[plane(dx, dy)],
                    dst_ref=drecv.at[dx * NY + dy],
                    send_sem=d_send.at[dx * NY + dy],
                    recv_sem=d_recv.at[dx * NY + dy],
                    device_id=(plane(dx, dy) * 2 + core, z),
                    device_id_type=MESH,
                )

            for dx, dy in STEPS:
                to = plane(dx, dy)
                dsend[to] = (halves[core, to] + sib[to]).astype(BF16)
                scatter(dx, dy).start()
            mine = halves[core, chip] + sib[chip]

    stores = [
        pltpu.make_async_copy(src, dst, out_sem.at[i])
        for i, (src, dst) in enumerate(((gg, gate_grad), (ug, up_grad), (dg, down_grad)))
    ]
    for store in stores:
        store.start()
    for dx, dy in reversed(STEPS):
        scatter(dx, dy).wait_recv()
        mine += drecv[dx * NY + dy].astype(F32)
    mixed[...] = mine[0:8].astype(BF16)
    input_grad[...] = mine[8:16].astype(BF16)
    for dx, dy in STEPS:
        gather(dx, dy, x, y).wait_send()
        scatter(dx, dy).wait_send()
    for dx in COLUMNS:
        forward(dx, core).wait_send()
    for u in range(LANES):
        for k in index:
            sum_copy(u, k).wait_send()
            spread_copy(u, k, z).wait_send()
    half.wait_send()
    for store in stores:
        store.wait()


LANES_FIRST = 0


def shards(tokens, gate_weight, up_weight, down_weight, out_grad):
    order, _ = plan(SUM_TREES, SPREAD_TREES)
    whole, anywhere = pl.BlockSpec(memory_space=pltpu.VMEM), pl.BlockSpec(memory_space=pl.ANY)
    dma = pltpu.SemaphoreType.DMA
    shape = jax.ShapeDtypeStruct
    outs = pl.pallas_call(
        functools.partial(kernel, SUM_TREES, SPREAD_TREES, order),
        out_shape=(
            shape((8, 512), BF16),
            shape((8, 512), BF16),
            shape((512, 768), BF16),
            shape((512, 768), BF16),
            shape((768, 512), BF16),
        ),
        in_specs=[whole, anywhere, anywhere, anywhere, whole],
        out_specs=(whole, whole, anywhere, anywhere, anywhere),
        scratch_shapes=[
            pltpu.VMEM((512, 768), BF16),
            pltpu.VMEM((512, 768), BF16),
            pltpu.VMEM((768, 512), BF16),
            pltpu.VMEM((2, NX, NY, 16, 512), BF16),
            pltpu.VMEM((256, 512), BF16),
            pltpu.VMEM((256, 512), BF16),
            pltpu.VMEM((LANES, NZ, 16, 3 * W), F32),
            pltpu.VMEM((LANES, NZ - 1, 16, 3 * W), F32),
            pltpu.VMEM((LANES, NZ, 16, 3 * W), BF16),
            pltpu.VMEM((2, 16, 16, 512), F32),
            pltpu.VMEM((16, 16, 512), F32),
            pltpu.VMEM((16, 16, 512), BF16),
            pltpu.VMEM((16, 16, 512), BF16),
            pltpu.VMEM((512, 768), BF16),
            pltpu.VMEM((512, 768), BF16),
            pltpu.VMEM((768, 512), BF16),
            dma((3,)), dma((3,)),
            dma((16,)), dma((16,)), dma((4,)), dma((4,)),
            dma((LANES, NZ - 1)), dma((LANES, NZ - 1)),
            dma((LANES, NZ - 1)), dma((LANES, NZ - 1)),
            dma, dma, dma((16,)), dma((16,)),
        ],
        compiler_params=pltpu.CompilerParams(
            collective_id=0, has_side_effects=True, vmem_limit_bytes=48 * 2**20
        ),
    )(tokens, gate_weight, up_weight, down_weight, out_grad)
    return outs


def solution(mesh):
    return jax.shard_map(
        shards,
        mesh=mesh,
        in_specs=(
            P("row", "col"),
            P("col", "row"),
            P("col", "row"),
            P("row", "col"),
            P("row", "col"),
        ),
        out_specs=(
            P("row", "col"),
            P("row", "col"),
            P("col", "row"),
            P("col", "row"),
            P("row", "col"),
        ),
        check_vma=False,
    )
```

time: 415 us -> 95.1 us (0.23)
  blocking collectives: 282 us -> 0 us
  waiting for transfers between devices: 99.8 us -> 0 us
  Pallas kernels: 0 us -> 85.5 us
  between operations: 14.1 us -> 0.66 us
  matrix products: 6.7 us -> 0 us
    psum x1 -> x0, blocking collectives: 160 us -> none  [reduce_rows(): summed = lax.psum(term_fn(0, total_rows), 'row')]
    all_gather x5 -> x0, blocking collectives: 122 us -> none  [the longest x1 29.3 us: shards(): lax.all_gather(out_grad, 'row', axis=0, tiled=True)]
    reduce_scatter x2 -> x0, waiting for transfers between devices: 99.7 us -> none  [the longest x1 72.6 us: shards(): lax.psum_scatter(jnp.dot(block, joined_weight, preferred_element_type=jnp...]
    pallas_call x0 -> x1, Pallas kernels: none -> 85.5 us  [shards(): pl.pallas_call(functools.partial(kernel, SUM_TREES, SPREAD_TREES, order),...]
    dot_general x5 -> x0, matrix products: 5.41 us -> none  [the longest x1 1.77 us: shards(): jnp.dot(block, joined_weight, preferred_element_type=jnp.float32)]
    unnamed x11 -> x15, local copies, waits for them, and re-layouts: 6.59 us -> 8.62 us
  transfers between devices with their start and end apart: 2 -> 0, of which waited for: 2 -> 0; matrix products, arithmetic and copies ran while one was open for 2% -> 0% of each run, Pallas kernels for 0% -> 0%
where the time goes in v1:
time: 95.1 us; the launch traced here: 94.8 us
  Pallas kernels  85.5 us (90%)
  local copies, waits for them, and re-layouts  8.62 us (9%)
    pallas_call x1, Pallas kernels, shards(): pl.pallas_call(functools.partial(kernel, SUM_TREES, SPREAD_TREES, order),...  85.5 us
    unnamed x15, local copies, waits for them, and re-layouts  8.62 us

profile of v1, /device:TPU:1, one launch (start us, length us, event | category | flops | bytes accessed | tf_op | source)
XLA Modules:
  0.0 94.8 jit_solution(5416246652317510023)
XLA Ops:
  0.6 0.0 copy-start
  0.6 1.1 %copy-done = bf16[512,768]{1,0:T(8,128)(2,1)S(1)} copy-done((bf16[512,768]{1,0:T(8,128)(2,1)S(1)}, bf16[512,768]{1,0:T(8,128)(2,1)}, u32[]{:S(2)}) %copy-start) | copy-done | bytes 786456
  1.8 0.0 copy-start.1
  1.8 1.1 %copy-done.1 = bf16[512,768]{1,0:T(8,128)(2,1)S(1)} copy-done((bf16[512,768]{1,0:T(8,128)(2,1)S(1)}, bf16[512,768]{1,0:T(8,128)(2,1)}, u32[]{:S(2)}) %copy-start.1) | copy-done | bytes 786456
  2.9 0.0 copy-start.2
  2.9 1.1 %copy-done.2 = bf16[768,512]{1,0:T(8,128)(2,1)S(1)} copy-done((bf16[768,512]{1,0:T(8,128)(2,1)S(1)}, bf16[768,512]{1,0:T(8,128)(2,1)}, u32[]{:S(2)}) %copy-start.2) | copy-done | bytes 786456
  4.0 0.0 copy-start.3
  4.0 0.7 copy-done.3
  4.7 0.0 copy-start.4
  4.7 0.7 copy-done.4
  5.4 85.5 %shard_map.92 = (bf16[8,512]{1,0:T(8,128)(2,1)S(1)}, bf16[8,512]{1,0:T(8,128)(2,1)S(1)}, bf16[512,768]{1,0:T(8,128)(2,1)S(1)}, bf16[512,768]{1,0:T(8,128)(2,1)S(1)}, bf16[768,512]{1,0:T(8,128)(2,1)S(1)}) custom-call(bf16[8,512]{1,0:T(8,128)(2,1)S(1)} %copy-done.3, bf16[512,768]{1,0:T(8,128)(2,1)S(1)} %copy-done, bf16[512,768]{1,0:T(8,128)(2,1)S(1)} %copy-done.1, ...), custom_call_target="tpu_custom_call" | custom-call | tf_op jit(solution)/shard_map/pallas_call | solution.py:344
  91.0 0.6 copy.15
  91.6 0.6 copy.16
  92.2 0.9 copy.17
  93.1 0.9 copy.18
  93.9 0.9 copy.19
Async XLA Ops:
  0.6 1.1 %copy-start = (bf16[512,768]{1,0:T(8,128)(2,1)S(1)}, bf16[512,768]{1,0:T(8,128)(2,1)}, u32[]{:S(2)}) copy-start(bf16[512,768]{1,0:T(8,128)(2,1)} %gate_w.1) | copy-start | bytes 2359300
  1.8 1.1 %copy-start.1 = (bf16[512,768]{1,0:T(8,128)(2,1)S(1)}, bf16[512,768]{1,0:T(8,128)(2,1)}, u32[]{:S(2)}) copy-start(bf16[512,768]{1,0:T(8,128)(2,1)} %up_w.1) | copy-start | bytes 2359300
  2.9 1.1 %copy-start.2 = (bf16[768,512]{1,0:T(8,128)(2,1)S(1)}, bf16[768,512]{1,0:T(8,128)(2,1)}, u32[]{:S(2)}) copy-start(bf16[768,512]{1,0:T(8,128)(2,1)} %down_w.1) | copy-start | bytes 2359300
  4.0 0.7 copy-start.3
  4.7 0.7 copy-start.4

commit v2 on v1

--- a/solution.py
+++ b/solution.py
@@ -12,21 +12,37 @@
 NZ, NX, NY = 16, 4, 4
 LANES, W = 3, 256
 
-RIGHT = {1: 0, 2: 1, 3: 2, 4: 3, 5: 4, 6: 5, 7: 6, 8: 7}
-LEFT = {-1: 0, -2: -1, -3: -2, -4: -3, -5: -4, -6: -5, -7: -6}
-SUM_TREES = [{**RIGHT, **LEFT}] * LANES
-SPREAD_TREES = [{**RIGHT, **LEFT}] * LANES
-
-
-def mirrored(tree):
-    return {-k: -p for k, p in tree.items()}
+SUM_FAR = {1: 0, 2: 1, 3: 2, 4: 3, 5: 6, 6: 2, 7: 6, 8: 6}
+SUM_NEAR = {1: 0, 2: 1, 3: 2, 4: 5, 5: 1, 6: 5, 7: 5}
+WIDE_FAR, WIDE_NEAR = (1, 2), (1,)
+SPREAD_FAR = {1: 0, 2: 1, 3: 4, 4: 0, 5: 4, 6: 4, 7: 6, 8: 6}
+SPREAD_NEAR = {1: 0, 2: 1, 3: 4, 4: 0, 5: 4, 6: 4, 7: 6}
+RATE, FIXED, HOP = 85.0, 2.35, 0.65
+
+
+def two_sided(far, near, way):
+    return {**{way * k: way * p for k, p in far.items()}, **{-way * k: -way * p for k, p in near.items()}}
+
+
+def sides(u):
+    return 1 if u % 2 == 0 else -1
+
+
+def trees():
+    sums = [two_sided(SUM_FAR, SUM_NEAR, sides(u)) for u in range(LANES)]
+    wide = [
+        {sides(u) * k for k in WIDE_FAR} | {-sides(u) * k for k in WIDE_NEAR} for u in range(LANES)
+    ]
+    spreads = [two_sided(SPREAD_FAR, SPREAD_NEAR, -sides(u)) for u in range(LANES)]
+    return sums, wide, spreads
 
 
 def children(tree, k):
     return [c for c, p in tree.items() if p == k]
 
 
-def plan(sum_trees, spread_trees, sum_kb=48.0, spread_kb=24.0):
+def plan(sum_trees, wide, spread_trees):
+    kb = 72.0 / LANES
     free = {1: 0.0, -1: 0.0}
     arrive = {}
     clock = 0.0
@@ -35,10 +51,10 @@
     def send(key, dist, kb, now):
         way = 1 if dist > 0 else -1
         hops = abs(dist)
-        wire = kb * 2 * hops / 112.0
+        wire = kb * 2 * hops / RATE
         begin = max(free[way], now)
         free[way] = begin + wire
-        arrive[key] = begin + wire + 2.2 + 0.6 * hops
+        arrive[key] = begin + wire + FIXED + HOP * hops
 
     todo = []
     for u in range(LANES):
@@ -49,7 +65,7 @@
         todo.append(("fin", u, 0))
         todo.append(("grad", u, 0))
     done = set()
-    cost = {"mm": 0.8, "sum": 0.15, "own": 0.4, "spread": 0.08, "fin": 0.8, "grad": 0.9}
+    cost = {"mm": 0.33, "sum": 0.06, "own": 0.1, "spread": 0.04, "fin": 0.3, "grad": 0.17}
     last = {"mm": 0, "grad": 1e6}
 
     def ready(task):
@@ -78,17 +94,17 @@
             at = ready(task)
             if at is None:
                 continue
-            rank = (max(at, clock) + last.get(task[0], 0.0) * 1.0, task[1], at)
+            rank = (max(at, clock) + last.get(task[0], 0.0), task[1], at)
             if best is None or rank < best[0]:
                 best = (rank, task, at)
         _, task, at = best
         kind, u, k = task
         clock = max(clock, at) + cost[kind]
         if kind == "sum":
-            send(("sum", u, k), k - sum_trees[u][k], sum_kb, clock)
+            send(("sum", u, k), k - sum_trees[u][k], kb * (2 if k in wide[u] else 1), clock)
         elif kind in ("own", "spread"):
             for c in children(spread_trees[u], k):
-                send(("spread", u, c), c - k, spread_kb, clock)
+                send(("spread", u, c), c - k, kb, clock)
         order.append(task)
         done.add(task)
         todo.remove(task)
@@ -124,10 +140,10 @@
 
 
 def kernel(
-    sum_trees, spread_trees, order,
+    sum_trees, wide, spread_trees, order,
     tok, gate_w, up_w, down_w, og,
     mixed, input_grad, gate_grad, up_grad, down_grad,
-    gw, uw, dw, slabs, xs, gs, part, slot, acts, halves, sib, dsend, drecv, gg, ug, dg,
+    gw, uw, dw, slabs, xs, gs, part, slot, low_out, low_in, acts, halves, sib, dsend, drecv, gg, ug, dg,
     w_sem, out_sem, a_send, a_recv, f_send, f_recv,
     sum_send, sum_recv, spread_send, spread_recv, h_send, h_recv, d_send, d_recv,
 ):
@@ -184,7 +200,7 @@
         gather(dx, dy, x, y).start()
     for dx in COLUMNS:
         for dy in range(NY):
-            if (dx, dy) != (0, 0):
+            if (dx, dy) in STEPS:
                 gather(dx, dy, (x - dx) % NX, (y - dy) % NY).wait_recv()
         forward(dx, core).start()
     for load in loads:
@@ -195,29 +211,39 @@
     xs[...] = both[:, :, :, 0:8, :].reshape(256, 512).astype(BF16)
     gs[...] = both[:, :, :, 8:16, :].reshape(256, 512).astype(BF16)
 
-    index = {k: i for i, k in enumerate(sorted(sum_trees[0]))}
+    def index(tree, k):
+        return sorted(tree).index(k)
 
     def sum_copy(u, k):
         o = k - sum_trees[u][k]
+        i = index(sum_trees[u], k)
         return pltpu.make_async_remote_copy(
-            src_ref=part.at[u, (z + k) % NZ],
-            dst_ref=slot.at[u, index[k]],
-            send_sem=sum_send.at[u, index[k]],
-            recv_sem=sum_recv.at[u, index[k]],
+            src_ref=part.at[u, (z + k) % NZ] if k in wide[u] else low_out.at[u, i],
+            dst_ref=slot.at[u, i] if k in wide[u] else low_in.at[u, i],
+            send_sem=sum_send.at[u, i],
+            recv_sem=sum_recv.at[u, i],
             device_id=(row, (z + o) % NZ),
             device_id_type=MESH,
         )
 
     def spread_copy(u, c, chunk):
         o = c - spread_trees[u][c]
+        i = index(spread_trees[u], c)
         return pltpu.make_async_remote_copy(
             src_ref=acts.at[u, chunk],
             dst_ref=acts.at[u, chunk],
-            send_sem=spread_send.at[u, index[c]],
-            recv_sem=spread_recv.at[u, index[c]],
+            send_sem=spread_send.at[u, i],
+            recv_sem=spread_recv.at[u, i],
             device_id=(row, (z + o) % NZ),
             device_id_type=MESH,
         )
+
+    def gathered(u, k, total):
+        for c in children(sum_trees[u], k):
+            sum_copy(u, c).wait_recv()
+            i = index(sum_trees[u], c)
+            total += slot[u, i] if c in wide[u] else low_in[u, i].astype(F32)
+        return total
 
     def spread_wait(u, k):
         spread_copy(u, k, (z - k) % NZ).wait_recv()
@@ -229,20 +255,15 @@
             part[u, :, :, W : 2 * W] = dot(xs[...], uw[:, unit], NN).reshape(NZ, 16, W)
             part[u, :, :, 2 * W : 3 * W] = dot(gs[...], dw[unit, :], NT).reshape(NZ, 16, W)
         elif kind == "sum":
-            below = children(sum_trees[u], k)
-            if below:
-                chunk = (z + k) % NZ
-                total = part[u, chunk]
-                for c in below:
-                    sum_copy(u, c).wait_recv()
-                    total += slot[u, index[c]]
+            chunk = (z + k) % NZ
+            total = gathered(u, k, part[u, chunk])
+            if k not in wide[u]:
+                low_out[u, index(sum_trees[u], k)] = total.astype(BF16)
+            elif children(sum_trees[u], k):
                 part[u, chunk] = total
             sum_copy(u, k).start()
         elif kind == "own":
-            total = part[u, z]
-            for c in children(sum_trees[u], 0):
-                sum_copy(u, c).wait_recv()
-                total += slot[u, index[c]]
+            total = gathered(u, 0, part[u, z])
             gate, up, hidden_grad = total[:, 0:W], total[:, W : 2 * W], total[:, 2 * W :]
             sig = jax.nn.sigmoid(gate)
             swish = gate * sig
@@ -325,8 +346,9 @@
     for dx in COLUMNS:
         forward(dx, core).wait_send()
     for u in range(LANES):
-        for k in index:
+        for k in sum_trees[u]:
             sum_copy(u, k).wait_send()
+        for k in spread_trees[u]:
             spread_copy(u, k, z).wait_send()
     half.wait_send()
     for store in stores:
@@ -336,13 +358,37 @@
 LANES_FIRST = 0
 
 
+def hand_on(pieces, *refs):
+    sources, targets, held, (in_sem, out_sem) = refs[:5], refs[5:10], refs[10:15], refs[15:]
+
+    def rows(ref, j, n):
+        return ref if n == ref.shape[0] else ref.at[pl.ds(j * n, n)]
+
+    loads = [
+        pltpu.make_async_copy(rows(sources[i], j, n), rows(held[i], j, n), in_sem.at[p])
+        for p, (i, j, n) in enumerate(pieces)
+    ]
+    stores = [
+        pltpu.make_async_copy(rows(held[i], j, n), rows(targets[i], j, n), out_sem.at[p])
+        for p, (i, j, n) in enumerate(pieces)
+    ]
+    for load in loads:
+        load.start()
+    for load, store in zip(loads, stores):
+        load.wait()
+        store.start()
+    for store in stores:
+        store.wait()
+
+
 def shards(tokens, gate_weight, up_weight, down_weight, out_grad):
-    order, _ = plan(SUM_TREES, SPREAD_TREES)
+    sum_trees, wide, spread_trees = trees()
+    order, _ = plan(sum_trees, wide, spread_trees)
     whole, anywhere = pl.BlockSpec(memory_space=pltpu.VMEM), pl.BlockSpec(memory_space=pl.ANY)
     dma = pltpu.SemaphoreType.DMA
     shape = jax.ShapeDtypeStruct
     outs = pl.pallas_call(
-        functools.partial(kernel, SUM_TREES, SPREAD_TREES, order),
+        functools.partial(kernel, sum_trees, wide, spread_trees, order),
         out_shape=(
             shape((8, 512), BF16),
             shape((8, 512), BF16),
@@ -361,6 +407,8 @@
             pltpu.VMEM((256, 512), BF16),
             pltpu.VMEM((LANES, NZ, 16, 3 * W), F32),
             pltpu.VMEM((LANES, NZ - 1, 16, 3 * W), F32),
+            pltpu.VMEM((LANES, NZ - 1, 16, 3 * W), BF16),
+            pltpu.VMEM((LANES, NZ - 1, 16, 3 * W), BF16),
             pltpu.VMEM((LANES, NZ, 16, 3 * W), BF16),
             pltpu.VMEM((2, 16, 16, 512), F32),
             pltpu.VMEM((16, 16, 512), F32),
@@ -376,10 +424,19 @@
             dma, dma, dma((16,)), dma((16,)),
         ],
         compiler_params=pltpu.CompilerParams(
-            collective_id=0, has_side_effects=True, vmem_limit_bytes=48 * 2**20
+            collective_id=0, has_side_effects=True, vmem_limit_bytes=62 * 2**20
         ),
     )(tokens, gate_weight, up_weight, down_weight, out_grad)
-    return outs
+    pieces = [(i, 0, o.shape[0]) for i, o in enumerate(outs[:2])]
+    pieces += [(i, j, o.shape[0] // 4) for i, o in enumerate(outs) if i > 1 for j in range(4)]
+    return pl.pallas_call(
+        functools.partial(hand_on, pieces),
+        out_shape=tuple(shape(o.shape, o.dtype) for o in outs),
+        in_specs=[anywhere] * 5,
+        out_specs=(anywhere,) * 5,
+        scratch_shapes=[pltpu.VMEM(o.shape, o.dtype) for o in outs]
+        + [dma((len(pieces),)), dma((len(pieces),))],
+    )(*outs)
 
 
 def solution(mesh):

time: 95.1 us -> 81.8 us (0.86)
  local copies, waits for them, and re-layouts: 8.62 us -> 0 us
  Pallas kernels: 85.5 us -> 80.8 us
    unnamed x15 -> x0, local copies, waits for them, and re-layouts: 8.62 us -> none
    pallas_call x1 -> x2, Pallas kernels: 85.5 us -> 80.8 us  [the longest x1 78.2 us: shards(): pl.pallas_call(functools.partial(kernel, sum_trees, wide, spread_trees, o...]
where the time goes in v2:
time: 81.8 us; the launch traced here: 81.5 us
  Pallas kernels  80.8 us (99%)
    pallas_call x1, Pallas kernels, shards(): pl.pallas_call(functools.partial(kernel, sum_trees, wide, spread_trees, o...  78.2 us
    pallas_call x1, Pallas kernels, shards(): pl.pallas_call(functools.partial(hand_on, pieces), out_shape=tuple((shape...  2.68 us

profile of v2, /device:TPU:1, one launch (start us, length us, event | category | flops | bytes accessed | tf_op | source)
XLA Modules:
  0.0 81.5 jit_solution(10232895895900474042)
XLA Ops:
  0.6 78.2 %shard_map.92 = (bf16[8,512]{1,0:T(8,128)(2,1)}, bf16[8,512]{1,0:T(8,128)(2,1)}, bf16[512,768]{1,0:T(8,128)(2,1)}, bf16[512,768]{1,0:T(8,128)(2,1)}, bf16[768,512]{1,0:T(8,128)(2,1)}) custom-call(bf16[8,512]{1,0:T(8,128)(2,1)} %tok.1, bf16[512,768]{1,0:T(8,128)(2,1)} %gate_w.1, bf16[512,768]{1,0:T(8,128)(2,1)} %up_w.1, bf16[768,512]{1,0:T(8,128)(2,1)} %down_w.1, ...), custom_call_target="tpu_custom_call" | custom-call | tf_op jit(solution)/shard_map/pallas_call | solution.py:390
  78.8 2.7 %shard_map.93 = (bf16[8,512]{1,0:T(8,128)(2,1)}, bf16[8,512]{1,0:T(8,128)(2,1)}, bf16[512,768]{1,0:T(8,128)(2,1)}, bf16[512,768]{1,0:T(8,128)(2,1)}, bf16[768,512]{1,0:T(8,128)(2,1)}) custom-call(bf16[8,512]{1,0:T(8,128)(2,1)} %get-tuple-element.10.refs_0_, bf16[8,512]{1,0:T(8,128)(2,1)} %get-tuple-element.11.refs_1_, ...), custom_call_target="tpu_custom_call" | custom-call | tf_op jit(solution)/shard_map/pallas_call | solution.py:432

commit v3 on v2

--- a/solution.py
+++ b/solution.py
@@ -12,12 +12,12 @@
 NZ, NX, NY = 16, 4, 4
 LANES, W = 3, 256
 
-SUM_FAR = {1: 0, 2: 1, 3: 2, 4: 3, 5: 6, 6: 2, 7: 6, 8: 6}
-SUM_NEAR = {1: 0, 2: 1, 3: 2, 4: 5, 5: 1, 6: 5, 7: 5}
-WIDE_FAR, WIDE_NEAR = (1, 2), (1,)
-SPREAD_FAR = {1: 0, 2: 1, 3: 4, 4: 0, 5: 4, 6: 4, 7: 6, 8: 6}
-SPREAD_NEAR = {1: 0, 2: 1, 3: 4, 4: 0, 5: 4, 6: 4, 7: 6}
-RATE, FIXED, HOP = 85.0, 2.35, 0.65
+SUM_FAR = {1: 0, 2: 1, 3: 2, 4: 3, 5: 6, 6: 3, 7: 6, 8: 6}
+SUM_NEAR = {1: 0, 2: 1, 3: 2, 4: 5, 5: 2, 6: 5, 7: 5}
+WIDE_FAR, WIDE_NEAR = (1, 2, 3), (1, 2)
+SPREAD_FAR = {1: 0, 2: 3, 3: 0, 4: 3, 5: 6, 6: 3, 7: 6, 8: 6}
+SPREAD_NEAR = {1: 0, 2: 3, 3: 0, 4: 3, 5: 3, 6: 5, 7: 5}
+RATE, BURST, FIXED, HOP = 95.0, 130.0, 2.35, 0.65
 
 
 def two_sided(far, near, way):
@@ -38,7 +38,7 @@
 
 
 def children(tree, k):
-    return [c for c, p in tree.items() if p == k]
+    return sorted((c for c, p in tree.items() if p == k), key=lambda c: -abs(c - k))
 
 
 def plan(sum_trees, wide, spread_trees):
@@ -51,15 +51,14 @@
     def send(key, dist, kb, now):
         way = 1 if dist > 0 else -1
         hops = abs(dist)
-        wire = kb * 2 * hops / RATE
         begin = max(free[way], now)
-        free[way] = begin + wire
-        arrive[key] = begin + wire + FIXED + HOP * hops
+        free[way] = begin + kb * 2 * hops / RATE
+        arrive[key] = begin + kb * 2 / BURST + FIXED + HOP * hops
 
     todo = []
     for u in range(LANES):
         todo.append(("mm", u, 0))
-        todo += [("sum", u, k) for k in sum_trees[u]]
+        todo += [("sum", u, k) for k in sorted(sum_trees[u], key=lambda k: -abs(k - sum_trees[u][k]))]
         todo.append(("own", u, 0))
         todo += [("spread", u, k) for k in spread_trees[u] if children(spread_trees[u], k)]
         todo.append(("fin", u, 0))
@@ -143,7 +142,7 @@
     sum_trees, wide, spread_trees, order,
     tok, gate_w, up_w, down_w, og,
     mixed, input_grad, gate_grad, up_grad, down_grad,
-    gw, uw, dw, slabs, xs, gs, part, slot, low_out, low_in, acts, halves, sib, dsend, drecv, gg, ug, dg,
+    own, mine, gw, uw, dw, slabs, xs, gs, part, slot, low_out, low_in, acts, halves, sib, dsend, drecv, gg, ug, dg,
     w_sem, out_sem, a_send, a_recv, f_send, f_recv,
     sum_send, sum_recv, spread_send, spread_recv, h_send, h_recv, d_send, d_recv,
 ):
@@ -152,13 +151,6 @@
     x, y = chip // NY, chip % NY
     sibling = (chip * 2 + 1 - core, z)
 
-    loads = [
-        pltpu.make_async_copy(src, dst, w_sem.at[i])
-        for i, (src, dst) in enumerate(((gate_w, gw), (up_w, uw), (down_w, dw)))
-    ]
-    for load in loads:
-        load.start()
-
     def plane(dx, dy):
         return ((x + dx) % NX) * NY + (y + dy) % NY
 
@@ -171,9 +163,17 @@
     for o in around:
         pl.semaphore_signal(barrier, inc=1, device_id=(row, (z + o) % NZ), device_id_type=MESH)
     pl.semaphore_signal(barrier, inc=1, device_id=sibling, device_id_type=MESH)
-    slabs[core, x, y] = jnp.concatenate(
-        [tok[...].astype(F32), og[...].astype(F32)], axis=0
-    ).astype(BF16)
+    loads = [
+        pltpu.make_async_copy(src, dst, w_sem.at[i])
+        for i, (src, dst) in enumerate(
+            ((gate_w, gw), (up_w, uw), (down_w, dw), (tok, own.at[0]), (og, own.at[1]))
+        )
+    ]
+    for load in reversed(loads):
+        load.start()
+    for load in loads[3:]:
+        load.wait()
+    slabs[core, x, y] = jnp.concatenate([own[0].astype(F32), own[1].astype(F32)], axis=0).astype(BF16)
     pl.semaphore_wait(barrier, len(STEPS) + len(around) + 1)
 
     def gather(dx, dy, from_x, from_y):
@@ -203,7 +203,7 @@
             if (dx, dy) in STEPS:
                 gather(dx, dy, (x - dx) % NX, (y - dy) % NY).wait_recv()
         forward(dx, core).start()
-    for load in loads:
+    for load in loads[:3]:
         load.wait()
     for dx in COLUMNS:
         forward(dx, 1 - core).wait_recv()
@@ -248,6 +248,7 @@
     def spread_wait(u, k):
         spread_copy(u, k, (z - k) % NZ).wait_recv()
 
+    begun = False
     for kind, u, k in order:
         unit = pl.ds(u * W, W)
         if kind == "mm":
@@ -289,11 +290,12 @@
             back = (dot(gate_delta, gw[:, unit], NT) + dot(up_delta, uw[:, unit], NT)).reshape(
                 2, 16, 8, 512
             )
-            if u != LANES_FIRST:
+            if begun:
                 out += halves[:, :, 0:8, :]
                 back += halves[:, :, 8:16, :]
             halves[:, :, 0:8, :] = out
             halves[:, :, 8:16, :] = back
+            begun = True
         else:
             hidden = acts[u, :, :, 0:W].reshape(256, W)
             gate_delta = acts[u, :, :, W : 2 * W].reshape(256, W)
@@ -327,22 +329,19 @@
                 to = plane(dx, dy)
                 dsend[to] = (halves[core, to] + sib[to]).astype(BF16)
                 scatter(dx, dy).start()
-            mine = halves[core, chip] + sib[chip]
 
     stores = [
         pltpu.make_async_copy(src, dst, out_sem.at[i])
-        for i, (src, dst) in enumerate(((gg, gate_grad), (ug, up_grad), (dg, down_grad)))
+        for i, (src, dst) in enumerate(
+            (
+                (gg, gate_grad), (ug, up_grad), (dg, down_grad), (mine.at[0], mixed), (mine.at[1], input_grad)
+            )
+        )
     ]
-    for store in stores:
+    for store in stores[:3]:
         store.start()
-    for dx, dy in reversed(STEPS):
-        scatter(dx, dy).wait_recv()
-        mine += drecv[dx * NY + dy].astype(F32)
-    mixed[...] = mine[0:8].astype(BF16)
-    input_grad[...] = mine[8:16].astype(BF16)
     for dx, dy in STEPS:
         gather(dx, dy, x, y).wait_send()
-        scatter(dx, dy).wait_send()
     for dx in COLUMNS:
         forward(dx, core).wait_send()
     for u in range(LANES):
@@ -351,11 +350,18 @@
         for k in spread_trees[u]:
             spread_copy(u, k, z).wait_send()
     half.wait_send()
+    total = halves[core, chip] + sib[chip]
+    for dx, dy in reversed(STEPS):
+        scatter(dx, dy).wait_recv()
+        total += drecv[dx * NY + dy].astype(F32)
+    mine[0] = total[0:8].astype(BF16)
+    mine[1] = total[8:16].astype(BF16)
+    for store in stores[3:]:
+        store.start()
+    for dx, dy in STEPS:
+        scatter(dx, dy).wait_send()
     for store in stores:
         store.wait()
-
-
-LANES_FIRST = 0
 
 
 def hand_on(pieces, *refs):
@@ -384,7 +390,7 @@
 def shards(tokens, gate_weight, up_weight, down_weight, out_grad):
     sum_trees, wide, spread_trees = trees()
     order, _ = plan(sum_trees, wide, spread_trees)
-    whole, anywhere = pl.BlockSpec(memory_space=pltpu.VMEM), pl.BlockSpec(memory_space=pl.ANY)
+    anywhere = pl.BlockSpec(memory_space=pl.ANY)
     dma = pltpu.SemaphoreType.DMA
     shape = jax.ShapeDtypeStruct
     outs = pl.pallas_call(
@@ -396,9 +402,11 @@
             shape((512, 768), BF16),
             shape((768, 512), BF16),
         ),
-        in_specs=[whole, anywhere, anywhere, anywhere, whole],
-        out_specs=(whole, whole, anywhere, anywhere, anywhere),
+        in_specs=[anywhere] * 5,
+        out_specs=(anywhere,) * 5,
         scratch_shapes=[
+            pltpu.VMEM((2, 8, 512), BF16),
+            pltpu.VMEM((2, 8, 512), BF16),
             pltpu.VMEM((512, 768), BF16),
             pltpu.VMEM((512, 768), BF16),
             pltpu.VMEM((768, 512), BF16),
@@ -417,7 +425,7 @@
             pltpu.VMEM((512, 768), BF16),
             pltpu.VMEM((512, 768), BF16),
             pltpu.VMEM((768, 512), BF16),
-            dma((3,)), dma((3,)),
+            dma((5,)), dma((5,)),
             dma((16,)), dma((16,)), dma((4,)), dma((4,)),
             dma((LANES, NZ - 1)), dma((LANES, NZ - 1)),
             dma((LANES, NZ - 1)), dma((LANES, NZ - 1)),

time: 81.8 us -> 80.9 us (0.989)
    pallas_call x1, Pallas kernels: 78.2 us -> 77.3 us  [shards(): pl.pallas_call(functools.partial(kernel, sum_trees, wide, spread_trees, o...]
where the time goes in v3:
time: 80.9 us; the launch traced here: 80.6 us
  Pallas kernels  80 us (99%)
    pallas_call x1, Pallas kernels, shards(): pl.pallas_call(functools.partial(kernel, sum_trees, wide, spread_trees, o...  77.3 us
    pallas_call x1, Pallas kernels, shards(): pl.pallas_call(functools.partial(hand_on, pieces), out_shape=tuple((shape...  2.68 us

profile of v3, /device:TPU:1, one launch (start us, length us, event | category | flops | bytes accessed | tf_op | source)
XLA Modules:
  0.0 80.6 jit_solution(9200564470036453950)
XLA Ops:
  0.6 77.3 %shard_map.92 = (bf16[8,512]{1,0:T(8,128)(2,1)}, bf16[8,512]{1,0:T(8,128)(2,1)}, bf16[512,768]{1,0:T(8,128)(2,1)}, bf16[512,768]{1,0:T(8,128)(2,1)}, bf16[768,512]{1,0:T(8,128)(2,1)}) custom-call(bf16[8,512]{1,0:T(8,128)(2,1)} %tok.1, bf16[512,768]{1,0:T(8,128)(2,1)} %gate_w.1, bf16[512,768]{1,0:T(8,128)(2,1)} %up_w.1, bf16[768,512]{1,0:T(8,128)(2,1)} %down_w.1, ...), custom_call_target="tpu_custom_call" | custom-call | tf_op jit(solution)/shard_map/pallas_call | solution.py:396
  78.0 2.7 %shard_map.93 = (bf16[8,512]{1,0:T(8,128)(2,1)}, bf16[8,512]{1,0:T(8,128)(2,1)}, bf16[512,768]{1,0:T(8,128)(2,1)}, bf16[512,768]{1,0:T(8,128)(2,1)}, bf16[768,512]{1,0:T(8,128)(2,1)}) custom-call(bf16[8,512]{1,0:T(8,128)(2,1)} %get-tuple-element.10.refs_0_, bf16[8,512]{1,0:T(8,128)(2,1)} %get-tuple-element.11.refs_1_, ...), custom_call_target="tpu_custom_call" | custom-call | tf_op jit(solution)/shard_map/pallas_call | solution.py:440

commit v4 on v3

--- a/solution.py
+++ b/solution.py
@@ -15,8 +15,8 @@
 SUM_FAR = {1: 0, 2: 1, 3: 2, 4: 3, 5: 6, 6: 3, 7: 6, 8: 6}
 SUM_NEAR = {1: 0, 2: 1, 3: 2, 4: 5, 5: 2, 6: 5, 7: 5}
 WIDE_FAR, WIDE_NEAR = (1, 2, 3), (1, 2)
-SPREAD_FAR = {1: 0, 2: 3, 3: 0, 4: 3, 5: 6, 6: 3, 7: 6, 8: 6}
-SPREAD_NEAR = {1: 0, 2: 3, 3: 0, 4: 3, 5: 3, 6: 5, 7: 5}
+SPREAD_FAR = {1: 0, 2: 0, 3: 2, 4: 2, 5: 4, 6: 4, 7: 6, 8: 6}
+SPREAD_NEAR = {1: 0, 2: 0, 3: 2, 4: 2, 5: 4, 6: 4, 7: 6}
 RATE, BURST, FIXED, HOP = 95.0, 130.0, 2.35, 0.65
 
 
@@ -203,13 +203,17 @@
             if (dx, dy) in STEPS:
                 gather(dx, dy, (x - dx) % NX, (y - dy) % NY).wait_recv()
         forward(dx, core).start()
+    def unpack(which):
+        rows, place = slabs[which].astype(F32), pl.ds(which * 128, 128)
+        xs[place, :] = rows[:, :, 0:8, :].reshape(128, 512).astype(BF16)
+        gs[place, :] = rows[:, :, 8:16, :].reshape(128, 512).astype(BF16)
+
+    unpack(core)
     for load in loads[:3]:
         load.wait()
     for dx in COLUMNS:
         forward(dx, 1 - core).wait_recv()
-    both = slabs[...].astype(F32)
-    xs[...] = both[:, :, :, 0:8, :].reshape(256, 512).astype(BF16)
-    gs[...] = both[:, :, :, 8:16, :].reshape(256, 512).astype(BF16)
+    unpack(1 - core)
 
     def index(tree, k):
         return sorted(tree).index(k)
@@ -304,16 +308,19 @@
             ug[:, unit] = dot(xs[...], up_delta, TN).astype(BF16)
             dg[unit, :] = dot(hidden, gs[...], TN).astype(BF16)
         if kind == "fin" and (kind, u, k) == [t for t in order if t[0] == "fin"][-1]:
-            half = pltpu.make_async_remote_copy(
-                src_ref=halves.at[1 - core],
-                dst_ref=sib,
-                send_sem=h_send,
-                recv_sem=h_recv,
-                device_id=sibling,
-                device_id_type=MESH,
-            )
-            half.start()
-            half.wait_recv()
+            def half(dx):
+                chips = pl.ds((x + dx) % NX * NY, NY)
+                return pltpu.make_async_remote_copy(
+                    src_ref=halves.at[1 - core, chips],
+                    dst_ref=sib.at[chips],
+                    send_sem=h_send.at[dx],
+                    recv_sem=h_recv.at[dx],
+                    device_id=sibling,
+                    device_id_type=MESH,
+                )
+
+            for dx in reversed(COLUMNS):
+                half(dx).start()
 
             def scatter(dx, dy):
                 return pltpu.make_async_remote_copy(
@@ -325,10 +332,13 @@
                     device_id_type=MESH,
                 )
 
-            for dx, dy in STEPS:
-                to = plane(dx, dy)
-                dsend[to] = (halves[core, to] + sib[to]).astype(BF16)
-                scatter(dx, dy).start()
+            for dx in reversed(COLUMNS):
+                half(dx).wait_recv()
+                for dy in (2, 1, 3, 0):
+                    if (dx, dy) in STEPS:
+                        to = plane(dx, dy)
+                        dsend[to] = (halves[core, to] + sib[to]).astype(BF16)
+                        scatter(dx, dy).start()
 
     stores = [
         pltpu.make_async_copy(src, dst, out_sem.at[i])
@@ -349,7 +359,8 @@
             sum_copy(u, k).wait_send()
         for k in spread_trees[u]:
             spread_copy(u, k, z).wait_send()
-    half.wait_send()
+    for dx in COLUMNS:
+        half(dx).wait_send()
     total = halves[core, chip] + sib[chip]
     for dx, dy in reversed(STEPS):
         scatter(dx, dy).wait_recv()
@@ -429,7 +440,7 @@
             dma((16,)), dma((16,)), dma((4,)), dma((4,)),
             dma((LANES, NZ - 1)), dma((LANES, NZ - 1)),
             dma((LANES, NZ - 1)), dma((LANES, NZ - 1)),
-            dma, dma, dma((16,)), dma((16,)),
+            dma((4,)), dma((4,)), dma((16,)), dma((16,)),
         ],
         compiler_params=pltpu.CompilerParams(
             collective_id=0, has_side_effects=True, vmem_limit_bytes=62 * 2**20

time: 80.9 us -> 79.3 us (0.980)
  Pallas kernels: 80 us -> 78.4 us
    pallas_call x1, Pallas kernels: 77.3 us -> 75.7 us  [shards(): pl.pallas_call(functools.partial(kernel, sum_trees, wide, spread_trees, o...]
where the time goes in v4:
time: 79.3 us; the launch traced here: 79.1 us
  Pallas kernels  78.4 us (99%)
    pallas_call x1, Pallas kernels, shards(): pl.pallas_call(functools.partial(kernel, sum_trees, wide, spread_trees, o...  75.7 us
    pallas_call x1, Pallas kernels, shards(): pl.pallas_call(functools.partial(hand_on, pieces), out_shape=tuple((shape...  2.68 us

profile of v4, /device:TPU:1, one launch (start us, length us, event | category | flops | bytes accessed | tf_op | source)
XLA Modules:
  0.0 79.1 jit_solution(14621356709592916768)
XLA Ops:
  0.6 75.7 %shard_map.92 = (bf16[8,512]{1,0:T(8,128)(2,1)}, bf16[8,512]{1,0:T(8,128)(2,1)}, bf16[512,768]{1,0:T(8,128)(2,1)}, bf16[512,768]{1,0:T(8,128)(2,1)}, bf16[768,512]{1,0:T(8,128)(2,1)}) custom-call(bf16[8,512]{1,0:T(8,128)(2,1)} %tok.1, bf16[512,768]{1,0:T(8,128)(2,1)} %gate_w.1, bf16[512,768]{1,0:T(8,128)(2,1)} %up_w.1, bf16[768,512]{1,0:T(8,128)(2,1)} %down_w.1, ...), custom_call_target="tpu_custom_call" | custom-call | tf_op jit(solution)/shard_map/pallas_call | solution.py:407
  76.4 2.7 %shard_map.93 = (bf16[8,512]{1,0:T(8,128)(2,1)}, bf16[8,512]{1,0:T(8,128)(2,1)}, bf16[512,768]{1,0:T(8,128)(2,1)}, bf16[512,768]{1,0:T(8,128)(2,1)}, bf16[768,512]{1,0:T(8,128)(2,1)}) custom-call(bf16[8,512]{1,0:T(8,128)(2,1)} %get-tuple-element.10.refs_0_, bf16[8,512]{1,0:T(8,128)(2,1)} %get-tuple-element.11.refs_1_, ...), custom_call_target="tpu_custom_call" | custom-call | tf_op jit(solution)/shard_map/pallas_call | solution.py:451

commit v5 on v4

--- a/solution.py
+++ b/solution.py
@@ -140,9 +140,9 @@
 
 def kernel(
     sum_trees, wide, spread_trees, order,
-    tok, gate_w, up_w, down_w, og,
+    rows, gate_w, up_w, down_w,
     mixed, input_grad, gate_grad, up_grad, down_grad,
-    own, mine, gw, uw, dw, slabs, xs, gs, part, slot, low_out, low_in, acts, halves, sib, dsend, drecv, gg, ug, dg,
+    mine, gw, uw, dw, slabs, xs, gs, part, slot, low_out, low_in, acts, halves, sib, dsend, drecv, gg, ug, dg,
     w_sem, out_sem, a_send, a_recv, f_send, f_recv,
     sum_send, sum_recv, spread_send, spread_recv, h_send, h_recv, d_send, d_recv,
 ):
@@ -166,14 +166,13 @@
     loads = [
         pltpu.make_async_copy(src, dst, w_sem.at[i])
         for i, (src, dst) in enumerate(
-            ((gate_w, gw), (up_w, uw), (down_w, dw), (tok, own.at[0]), (og, own.at[1]))
+            ((gate_w, gw), (up_w, uw), (down_w, dw), (rows, slabs.at[core, x, y]))
         )
     ]
     for load in reversed(loads):
         load.start()
     for load in loads[3:]:
         load.wait()
-    slabs[core, x, y] = jnp.concatenate([own[0].astype(F32), own[1].astype(F32)], axis=0).astype(BF16)
     pl.semaphore_wait(barrier, len(STEPS) + len(around) + 1)
 
     def gather(dx, dy, from_x, from_y):
@@ -375,27 +374,12 @@
         store.wait()
 
 
-def hand_on(pieces, *refs):
-    sources, targets, held, (in_sem, out_sem) = refs[:5], refs[5:10], refs[10:15], refs[15:]
-
-    def rows(ref, j, n):
-        return ref if n == ref.shape[0] else ref.at[pl.ds(j * n, n)]
-
-    loads = [
-        pltpu.make_async_copy(rows(sources[i], j, n), rows(held[i], j, n), in_sem.at[p])
-        for p, (i, j, n) in enumerate(pieces)
-    ]
-    stores = [
-        pltpu.make_async_copy(rows(held[i], j, n), rows(targets[i], j, n), out_sem.at[p])
-        for p, (i, j, n) in enumerate(pieces)
-    ]
-    for load in loads:
-        load.start()
-    for load, store in zip(loads, stores):
-        load.wait()
-        store.start()
-    for store in stores:
-        store.wait()
+def hand_on(*refs):
+    copies = [pltpu.make_async_copy(refs[i], refs[5 + i], refs[10].at[i]) for i in range(5)]
+    for copy in copies:
+        copy.start()
+    for copy in copies:
+        copy.wait()
 
 
 def shards(tokens, gate_weight, up_weight, down_weight, out_grad):
@@ -413,10 +397,9 @@
             shape((512, 768), BF16),
             shape((768, 512), BF16),
         ),
-        in_specs=[anywhere] * 5,
+        in_specs=[anywhere] * 4,
         out_specs=(anywhere,) * 5,
         scratch_shapes=[
-            pltpu.VMEM((2, 8, 512), BF16),
             pltpu.VMEM((2, 8, 512), BF16),
             pltpu.VMEM((512, 768), BF16),
             pltpu.VMEM((512, 768), BF16),
@@ -443,18 +426,16 @@
             dma((4,)), dma((4,)), dma((16,)), dma((16,)),
         ],
         compiler_params=pltpu.CompilerParams(
-            collective_id=0, has_side_effects=True, vmem_limit_bytes=62 * 2**20
+            collective_id=0, has_side_effects=True, vmem_limit_bytes=205 * 2**18
         ),
-    )(tokens, gate_weight, up_weight, down_weight, out_grad)
-    pieces = [(i, 0, o.shape[0]) for i, o in enumerate(outs[:2])]
-    pieces += [(i, j, o.shape[0] // 4) for i, o in enumerate(outs) if i > 1 for j in range(4)]
+    )(jnp.concatenate([tokens, out_grad], axis=0), gate_weight, up_weight, down_weight)
     return pl.pallas_call(
-        functools.partial(hand_on, pieces),
+        hand_on,
         out_shape=tuple(shape(o.shape, o.dtype) for o in outs),
-        in_specs=[anywhere] * 5,
+        in_specs=[pl.BlockSpec(memory_space=pltpu.VMEM)] * 5,
         out_specs=(anywhere,) * 5,
-        scratch_shapes=[pltpu.VMEM(o.shape, o.dtype) for o in outs]
-        + [dma((len(pieces),)), dma((len(pieces),))],
+        scratch_shapes=[dma((5,))],
+        compiler_params=pltpu.CompilerParams(vmem_limit_bytes=4 * 2**20),
     )(*outs)
 
 

time: 79.3 us -> 78.2 us (0.986)
  Pallas kernels: 78.4 us -> 76.7 us
    pallas_call x1, Pallas kernels: 2.68 us -> 1.45 us  [shards(): pl.pallas_call(hand_on, out_shape=tuple((shape(o.shape, o.dtype) for o in...]
where the time goes in v5:
time: 78.2 us; the launch traced here: 78 us
  Pallas kernels  76.7 us (98%)
    pallas_call x1, Pallas kernels, shards(): pl.pallas_call(functools.partial(kernel, sum_trees, wide, spread_trees, o...  75.2 us

profile of v5, /device:TPU:1, one launch (start us, length us, event | category | flops | bytes accessed | tf_op | source)
XLA Modules:
  0.0 78.0 jit_solution(17521437607593670479)
XLA Ops:
  0.6 0.7 pad_maximum_fusion.rows
  1.3 75.2 %shard_map.92 = (bf16[8,512]{1,0:T(8,128)(2,1)S(1)}, bf16[8,512]{1,0:T(8,128)(2,1)S(1)}, bf16[512,768]{1,0:T(8,128)(2,1)S(1)}, bf16[512,768]{1,0:T(8,128)(2,1)S(1)}, bf16[768,512]{1,0:T(8,128)(2,1)S(1)}) custom-call(bf16[16,512]{1,0:T(8,128)(2,1)S(1)} %pad_maximum_fusion.rows, bf16[512,768]{1,0:T(8,128)(2,1)} %gate_w.1, bf16[512,768]{1,0:T(8,128)(2,1)} %up_w.1, ...), custom_call_target="tpu_custom_call" | custom-call | tf_op jit(solution)/shard_map/pallas_call | solution.py:391
  76.6 1.5 %shard_map.93 = (bf16[8,512]{1,0:T(8,128)(2,1)}, bf16[8,512]{1,0:T(8,128)(2,1)}, bf16[512,768]{1,0:T(8,128)(2,1)}, bf16[512,768]{1,0:T(8,128)(2,1)}, bf16[768,512]{1,0:T(8,128)(2,1)}) custom-call(bf16[8,512]{1,0:T(8,128)(2,1)S(1)} %get-tuple-element.10.refs_0_, bf16[8,512]{1,0:T(8,128)(2,1)S(1)} %get-tuple-element.11.refs_1_, ...), custom_call_target="tpu_custom_call" | custom-call | tf_op jit(solution)/shard_map/pallas_call | solution.py:432

commit v6 on v5

--- a/solution.py
+++ b/solution.py
@@ -25,7 +25,7 @@
 
 
 def sides(u):
-    return 1 if u % 2 == 0 else -1
+    return 1 if u == 0 else -1
 
 
 def trees():
@@ -142,8 +142,8 @@
     sum_trees, wide, spread_trees, order,
     rows, gate_w, up_w, down_w,
     mixed, input_grad, gate_grad, up_grad, down_grad,
-    mine, gw, uw, dw, slabs, xs, gs, part, slot, low_out, low_in, acts, halves, sib, dsend, drecv, gg, ug, dg,
-    w_sem, out_sem, a_send, a_recv, f_send, f_recv,
+    gw, uw, dw, slabs, xs, gs, part, slot, low_out, low_in, acts, halves, sib, dsend, drecv,
+    w_sem, a_send, a_recv, f_send, f_recv,
     sum_send, sum_recv, spread_send, spread_recv, h_send, h_recv, d_send, d_recv,
 ):
     row, z = lax.axis_index("row"), lax.axis_index("col")
@@ -303,9 +303,9 @@
             hidden = acts[u, :, :, 0:W].reshape(256, W)
             gate_delta = acts[u, :, :, W : 2 * W].reshape(256, W)
             up_delta = acts[u, :, :, 2 * W : 3 * W].reshape(256, W)
-            gg[:, unit] = dot(xs[...], gate_delta, TN).astype(BF16)
-            ug[:, unit] = dot(xs[...], up_delta, TN).astype(BF16)
-            dg[unit, :] = dot(hidden, gs[...], TN).astype(BF16)
+            gate_grad[:, unit] = dot(xs[...], gate_delta, TN).astype(BF16)
+            up_grad[:, unit] = dot(xs[...], up_delta, TN).astype(BF16)
+            down_grad[unit, :] = dot(hidden, gs[...], TN).astype(BF16)
         if kind == "fin" and (kind, u, k) == [t for t in order if t[0] == "fin"][-1]:
             def half(dx):
                 chips = pl.ds((x + dx) % NX * NY, NY)
@@ -339,16 +339,6 @@
                         dsend[to] = (halves[core, to] + sib[to]).astype(BF16)
                         scatter(dx, dy).start()
 
-    stores = [
-        pltpu.make_async_copy(src, dst, out_sem.at[i])
-        for i, (src, dst) in enumerate(
-            (
-                (gg, gate_grad), (ug, up_grad), (dg, down_grad), (mine.at[0], mixed), (mine.at[1], input_grad)
-            )
-        )
-    ]
-    for store in stores[:3]:
-        store.start()
     for dx, dy in STEPS:
         gather(dx, dy, x, y).wait_send()
     for dx in COLUMNS:
@@ -364,14 +354,10 @@
     for dx, dy in reversed(STEPS):
         scatter(dx, dy).wait_recv()
         total += drecv[dx * NY + dy].astype(F32)
-    mine[0] = total[0:8].astype(BF16)
-    mine[1] = total[8:16].astype(BF16)
-    for store in stores[3:]:
-        store.start()
+    mixed[...] = total[0:8].astype(BF16)
+    input_grad[...] = total[8:16].astype(BF16)
     for dx, dy in STEPS:
         scatter(dx, dy).wait_send()
-    for store in stores:
-        store.wait()
 
 
 def hand_on(*refs):
@@ -398,9 +384,8 @@
             shape((768, 512), BF16),
         ),
         in_specs=[anywhere] * 4,
-        out_specs=(anywhere,) * 5,
+        out_specs=(pl.BlockSpec(memory_space=pltpu.VMEM),) * 5,
         scratch_shapes=[
-            pltpu.VMEM((2, 8, 512), BF16),
             pltpu.VMEM((512, 768), BF16),
             pltpu.VMEM((512, 768), BF16),
             pltpu.VMEM((768, 512), BF16),
@@ -416,10 +401,7 @@
             pltpu.VMEM((16, 16, 512), F32),
             pltpu.VMEM((16, 16, 512), BF16),
             pltpu.VMEM((16, 16, 512), BF16),
-            pltpu.VMEM((512, 768), BF16),
-            pltpu.VMEM((512, 768), BF16),
-            pltpu.VMEM((768, 512), BF16),
-            dma((5,)), dma((5,)),
+            dma((5,)),
             dma((16,)), dma((16,)), dma((4,)), dma((4,)),
             dma((LANES, NZ - 1)), dma((LANES, NZ - 1)),
             dma((LANES, NZ - 1)), dma((LANES, NZ - 1)),

time: 78.2 us -> 79.1 us (1.012)
  Pallas kernels: 76.7 us -> 77.5 us
    pallas_call x1, Pallas kernels: 75.2 us -> 76.1 us  [shards(): pl.pallas_call(functools.partial(kernel, sum_trees, wide, spread_trees, o...]
where the time goes in v6:
time: 79.1 us; the launch traced here: 78.9 us
  Pallas kernels  77.5 us (98%)
    pallas_call x1, Pallas kernels, shards(): pl.pallas_call(functools.partial(kernel, sum_trees, wide, spread_trees, o...  76.1 us

profile of v6, /device:TPU:1, one launch (start us, length us, event | category | flops | bytes accessed | tf_op | source)
XLA Modules:
  0.0 78.9 jit_solution(949469698108549304)
XLA Ops:
  0.6 0.7 pad_maximum_fusion.rows
  1.3 76.1 %shard_map.92 = (bf16[8,512]{1,0:T(8,128)(2,1)S(1)}, bf16[8,512]{1,0:T(8,128)(2,1)S(1)}, bf16[512,768]{1,0:T(8,128)(2,1)S(1)}, bf16[512,768]{1,0:T(8,128)(2,1)S(1)}, bf16[768,512]{1,0:T(8,128)(2,1)S(1)}) custom-call(bf16[16,512]{1,0:T(8,128)(2,1)S(1)} %pad_maximum_fusion.rows, bf16[512,768]{1,0:T(8,128)(2,1)} %gate_w.1, bf16[512,768]{1,0:T(8,128)(2,1)} %up_w.1, ...), custom_call_target="tpu_custom_call" | custom-call | tf_op jit(solution)/shard_map/pallas_call | solution.py:377
  77.4 1.5 %shard_map.93 = (bf16[8,512]{1,0:T(8,128)(2,1)}, bf16[8,512]{1,0:T(8,128)(2,1)}, bf16[512,768]{1,0:T(8,128)(2,1)}, bf16[512,768]{1,0:T(8,128)(2,1)}, bf16[768,512]{1,0:T(8,128)(2,1)}) custom-call(bf16[8,512]{1,0:T(8,128)(2,1)S(1)} %get-tuple-element.10.refs_0_, bf16[8,512]{1,0:T(8,128)(2,1)S(1)} %get-tuple-element.11.refs_1_, ...), custom_call_target="tpu_custom_call" | custom-call | tf_op jit(solution)/shard_map/pallas_call | solution.py:414

commit v7 on v6

--- a/solution.py
+++ b/solution.py
@@ -25,7 +25,7 @@
 
 
 def sides(u):
-    return 1 if u == 0 else -1
+    return 1 if u % 2 == 0 else -1
 
 
 def trees():

time: 79.1 us -> 78.1 us (0.987)
  Pallas kernels: 77.5 us -> 76.6 us
    pallas_call x1, Pallas kernels: 76.1 us -> 75.1 us  [shards(): pl.pallas_call(functools.partial(kernel, sum_trees, wide, spread_trees, o...]
where the time goes in v7:
time: 78.1 us; the launch traced here: 77.9 us
  Pallas kernels  76.6 us (98%)
    pallas_call x1, Pallas kernels, shards(): pl.pallas_call(functools.partial(kernel, sum_trees, wide, spread_trees, o...  75.1 us

profile of v7, /device:TPU:1, one launch (start us, length us, event | category | flops | bytes accessed | tf_op | source)
XLA Modules:
  0.0 77.9 jit_solution(11580818508115299896)
XLA Ops:
  0.6 0.7 pad_maximum_fusion.rows
  1.3 75.1 %shard_map.92 = (bf16[8,512]{1,0:T(8,128)(2,1)S(1)}, bf16[8,512]{1,0:T(8,128)(2,1)S(1)}, bf16[512,768]{1,0:T(8,128)(2,1)S(1)}, bf16[512,768]{1,0:T(8,128)(2,1)S(1)}, bf16[768,512]{1,0:T(8,128)(2,1)S(1)}) custom-call(bf16[16,512]{1,0:T(8,128)(2,1)S(1)} %pad_maximum_fusion.rows, bf16[512,768]{1,0:T(8,128)(2,1)} %gate_w.1, bf16[512,768]{1,0:T(8,128)(2,1)} %up_w.1, ...), custom_call_target="tpu_custom_call" | custom-call | tf_op jit(solution)/shard_map/pallas_call | solution.py:377
  76.5 1.5 %shard_map.93 = (bf16[8,512]{1,0:T(8,128)(2,1)}, bf16[8,512]{1,0:T(8,128)(2,1)}, bf16[512,768]{1,0:T(8,128)(2,1)}, bf16[512,768]{1,0:T(8,128)(2,1)}, bf16[768,512]{1,0:T(8,128)(2,1)}) custom-call(bf16[8,512]{1,0:T(8,128)(2,1)S(1)} %get-tuple-element.10.refs_0_, bf16[8,512]{1,0:T(8,128)(2,1)S(1)} %get-tuple-element.11.refs_1_, ...), custom_call_target="tpu_custom_call" | custom-call | tf_op jit(solution)/shard_map/pallas_call | solution.py:414
